TPU v7x, 32 devices: a whole 2x2x4 slice. The times are simulated.
32 devices in a mesh: groups: 1, expert: 8 (over z, y), dp: 4 (over x, core).
Axes of the slice: x: 2, y: 2, z: 4, core: 2. Of those that a mesh axis runs over, the one named last changes fastest.
Arguments:
- tokens: bfloat16 [256, 4096], P(('groups', 'expert', 'dp')), may hold values from -6 to 6
- norm_gain: float32 [4096], replicated, may hold values from 0.1 to 1.9
- gate_weight: bfloat16 [32, 4096, 384], P(('expert', 'dp')), may hold values from -0.09375 to 0.09375
- up_weight: bfloat16 [32, 4096, 384], P(('expert', 'dp')), may hold values from -0.09375 to 0.09375
- down_weight: bfloat16 [32, 384, 4096], P(('expert', 'dp')), may hold values from -0.21875 to 0.21875
- experts_chosen: int32 [256, 8], P(('groups', 'expert', 'dp')), may hold values from 0 to 15, all different within a row; in each aligned block of 8 rows (0 to 7, 8 to 15, ...) at most 5 rows name the same one
- replica_choice: int32 [256, 8], P(('groups', 'expert', 'dp')), may hold values from 0 to 3
- replica_cols: int32 [2, 4], replicated, may hold values from 0 to 7, as said below
- combine_weight: float32 [256, 8], P(('groups', 'expert', 'dp')), may hold values from 0.1 to 0.5
Outputs:
- mixed: bfloat16 [256, 4096], P(('groups', 'expert', 'dp'))
- loads: float32 [32, 2], P(('groups', 'expert', 'dp'))
Inputs may be any that keep to these rules, and one draw needn't show every extreme that they name: `experts_chosen`: in each device's 8 tokens no expert is named more than 5 times; a token names 8 different experts. `replica_cols`: each row names 4 different columns of the expert axis.
All inputs are finite; a program needn't handle non-finite values.
Results may differ from a plain program's by a relative error of at most 0.0072.
Values may be sent and summed in bfloat16 or wider, within the bound.
A program may use at most 64 MiB of HBM per device.

v0:
```python
import jax
import jax.numpy as jnp
from jax import lax
from jax.sharding import PartitionSpec as P


def expert_block(slot_rows, gate_piece, up_piece, down_piece):
    gate_out = jnp.dot(slot_rows, gate_piece, preferred_element_type=jnp.float32)
    up_out = jnp.dot(slot_rows, up_piece, preferred_element_type=jnp.float32)
    hidden = (jax.nn.silu(gate_out) * up_out).astype(jnp.bfloat16)
    return jnp.dot(hidden, down_piece, preferred_element_type=jnp.float32).astype(jnp.bfloat16)


def per_device(
    tokens,
    norm_gain,
    gate_weight,
    up_weight,
    down_weight,
    experts_chosen,
    replica_choice,
    replica_cols,
    combine_weight,
):
    expert_count = lax.axis_size("expert")
    dp_count = lax.axis_size("dp")
    devices = expert_count * dp_count
    pair_cols = dp_count // 2
    pair_count = devices // 2
    tok_rows, model_width = tokens.shape
    top_k = experts_chosen.shape[1]
    rep_count = replica_cols.shape[1]
    capacity = min(tok_rows, tok_rows * top_k // pair_count + 1)
    assigned = tok_rows * top_k
    values = tokens.astype(jnp.float32)
    scale = lax.rsqrt(jnp.mean(values * values, axis=1, keepdims=True) + 1e-06)
    normed = (values * scale * norm_gain).astype(jnp.bfloat16)
    flat_ids = experts_chosen.reshape(-1)
    flat_choice = replica_choice.reshape(-1)
    column = flat_ids // pair_cols
    within = flat_ids % pair_cols
    rows_hot = (within[:, None] == jnp.arange(pair_cols, dtype=jnp.int32)[None, :]).astype(
        jnp.int32
    )
    cols_hot = (flat_choice[:, None] == jnp.arange(rep_count, dtype=jnp.int32)[None, :]).astype(
        jnp.int32
    )
    home_col = jnp.sum(rows_hot * replica_cols[None, :, 0], axis=1)
    chosen_col = jnp.sum(
        rows_hot[:, :, None] * cols_hot[:, None, :] * replica_cols[None, :, :], axis=(1, 2)
    )
    holder_col = jnp.where(column == home_col, chosen_col, column)
    plan_slot = (holder_col != column).astype(jnp.int32)
    plan_pair = holder_col * pair_cols + within
    plan_key = plan_pair * 2 + plan_slot
    key_counts = jnp.sum(
        (plan_key[:, None] == jnp.arange(pair_count * 2, dtype=jnp.int32)[None, :]).astype(
            jnp.float32
        ),
        axis=0,
    )
    count_rows = jnp.broadcast_to(key_counts.reshape(pair_count, 1, 2), (pair_count, 2, 2)).reshape(
        devices, 2
    )
    served = lax.psum_scatter(count_rows, ("expert", "dp"), scatter_dimension=0, tiled=True)
    loads = served / jnp.float32(tok_rows)
    positions = jnp.arange(assigned, dtype=jnp.int32)
    matches = flat_ids[:, None] == flat_ids[None, :]
    earlier = positions[:, None] > positions[None, :]
    rank_in = jnp.sum((matches & earlier).astype(jnp.int32), axis=1)
    row_index = flat_ids * capacity + rank_in
    bucket_rows = pair_count * capacity
    selector = jnp.arange(bucket_rows, dtype=jnp.int32)[:, None] == row_index[None, :]
    filled = jnp.any(selector, axis=1)
    token_index = jnp.sum(jnp.where(selector, (positions // top_k)[None, :], 0), axis=1)
    gathered = jnp.where(filled[:, None], normed[token_index], jnp.zeros((), jnp.bfloat16))
    bucket = jnp.broadcast_to(
        gathered.reshape(pair_count, 1, capacity, model_width),
        (pair_count, 2, capacity, model_width),
    )
    bucket = bucket.reshape(devices, capacity, model_width)
    received = lax.all_to_all(bucket, ("expert", "dp"), split_axis=0, concat_axis=0, tiled=True)
    slot_rows = received.reshape(-1, model_width)
    result_rows = expert_block(slot_rows, gate_weight[0], up_weight[0], down_weight[0])
    returned = lax.all_to_all(
        result_rows.reshape(received.shape[0], received.shape[1], model_width),
        ("expert", "dp"),
        split_axis=0,
        concat_axis=0,
        tiled=True,
    )
    pair_result = returned.reshape(pair_count, 2, capacity, model_width).astype(jnp.float32)
    pair_result = jnp.sum(pair_result, axis=1).reshape(bucket_rows, model_width)
    per_assign = pair_result[row_index] * combine_weight.reshape(-1)[:, None]
    mixed = jnp.sum(per_assign.reshape(tok_rows, top_k, model_width), axis=1).astype(jnp.bfloat16)
    return (mixed, loads)


def solution(mesh):
    return jax.shard_map(
        per_device,
        mesh=mesh,
        in_specs=(
            P(("groups", "expert", "dp"), None),
            P(),
            P(("expert", "dp"), None, None),
            P(("expert", "dp"), None, None),
            P(("expert", "dp"), None, None),
            P(("groups", "expert", "dp"), None),
            P(("groups", "expert", "dp"), None),
            P(),
            P(("groups", "expert", "dp"), None),
        ),
        out_specs=(P(("groups", "expert", "dp"), None), P(("groups", "expert", "dp"), None)),
        check_vma=False,
    )
```

profile of v0, /device:TPU:0, one launch (start us, length us, event | category | flops | bytes accessed | tf_op | source)
XLA Modules:
  0.0 167.8 jit_solution(8613781989290599803)
XLA Ops:
  0.6 0.0 copy-start
  0.6 0.9 reshape.233
  1.6 0.2 convert_reduce_fusion.1
  1.8 0.8 eq.94
  2.5 0.8 slice_reduce_fusion
  3.3 0.1 select_reduce_fusion.1
  3.4 0.8 multiply_reduce_fusion
  4.2 0.1 fusion.23
  4.3 0.1 select_reduce_fusion
  4.4 1.0 fusion.19
  5.4 0.9 fusion.21
  6.4 1.8 %gather_fusion = bf16[80,4096]{1,0:T(8,128)(2,1)} fusion(bf16[8,4096]{1,0:T(8,128)(2,1)S(1)} %fusion.21, s32[1024]{0:T(1024)S(1)} %pad_clamp_fusion.1), kind=kCustom, calls=%fused_computation | custom fusion | bytes 1311040 | tf_op jit(solution)/shard_map/gather | solution.py:76
  8.2 2.3 %gather.11 = bf16[16,5,4096]{2,1,0:T(8,128)(2,1)} reshape(bf16[80,4096]{1,0:T(8,128)(2,1)} %gather_fusion) | data formatting | bytes 1310720 | tf_op jit(solution)/shard_map/gather | solution.py:76
  10.5 0.1 broadcast_in_dim.28
  10.6 1.4 broadcast_select_fusion
  12.0 0.2 broadcast_in_dim.37
  12.2 55.9 %all_to_all.10 = bf16[32,5,4096]{2,1,0:T(8,128)(2,1)} all-to-all(bf16[32,5,4096]{2,1,0:T(8,128)(2,1)S(1)} %bitcast.39), channel_id=1, replica_groups=mesh['groups'=1,'expert'=8,'dp'=4] {'expert','dp'}, dimensions={0} | all-to-all | bytes 2621440 | tf_op jit(solution)/shard_map/all_to_all | solution.py:82
  68.1 2.7 %reshape.235 = bf16[160,4096]{1,0:T(8,128)(2,1)} reshape(bf16[32,5,4096]{2,1,0:T(8,128)(2,1)} %all_to_all.10) | data formatting | bytes 2621440 | tf_op jit(solution)/shard_map/reshape | solution.py:83
  70.8 3.1 %fusion.3 = f32[160,384]{1,0:T(8,128)S(1)} fusion(bf16[160,4096]{1,0:T(8,128)(2,1)} %reshape.235, bf16[1,4096,384]{2,1,0:T(8,128)(2,1)} %param.11), kind=kOutput, calls=%fused_computation.7 | convolution fusion | flops 503316480 | bytes 4702208 | tf_op jit(solution)/shard_map/dot_general | solution.py:8
  74.0 0.0 copy-done
  74.0 5.0 %convolution_convert_fusion = bf16[160,4096]{1,0:T(8,128)(2,1)} fusion(bf16[1,384,4096]{2,1,0:T(8,128)(2,1)S(1)} %copy-done, bf16[160,4096]{1,0:T(8,128)(2,1)} %reshape.235, bf16[1,4096,384]{2,1,0:T(8,128)(2,1)} %param.12, f32[160,384]{1,0:T(8,128)S(1)} %fusion.3), kind=kOutput, calls=%fused_computation.2 | convolution fusion | flops 1007656960 | bytes 9158656 | tf_op jit(solution)/shard_map/dot_general | solution.py:11
  79.0 2.6 %reshape.236 = bf16[32,5,4096]{2,1,0:T(8,128)(2,1)} reshape(bf16[160,4096]{1,0:T(8,128)(2,1)} %convolution_convert_fusion) | data formatting | bytes 2621440 | tf_op jit(solution)/shard_map/reshape | solution.py:86
  81.6 0.0 copy-start.1
  81.6 3.8 %all-to-all-start.1 = ((bf16[32,5,4096]{2,1,0:T(8,128)(2,1)}), bf16[32,5,4096]{2,1,0:T(8,128)(2,1)}, u32[]{:S(2)}, u32[]{:S(2)}) async-start(bf16[32,5,4096]{2,1,0:T(8,128)(2,1)} %reshape.236), calls=%async_computation.1 | async-start | bytes 4194304 | tf_op jit(solution)/shard_map/all_to_all | solution.py:85
  85.4 0.0 copy-done.1
  85.5 0.1 mul.115
  85.5 0.1 convert_reduce_fusion.2
  85.6 0.1 broadcast_in_dim.38
  85.7 0.1 copy.17
  85.8 0.1 broadcast_in_dim.39
  85.9 0.1 reshape.238
  86.0 68.8 %all-reduce = f32[32,2]{0,1:T(2,128)S(1)} all-reduce(f32[32,2]{0,1:T(2,128)S(1)} %reshape.238), channel_id=2, replica_groups=mesh['groups'=1,'expert'=8,'dp'=4] {'expert','dp'}, use_global_device_ids=true, to_apply=%region_9.10.clone | all-reduce | flops 64 | bytes 512
  154.8 0.1 dynamic-slice_multiply_fusion
  154.8 0.6 copy.18
  155.4 0.0 all-to-all-done.1
  155.5 3.6 %convert_reduce_fusion = f32[16,5,4096]{2,1,0:T(8,128)} fusion(bf16[32,5,4096]{2,1,0:T(8,128)(2,1)} %all-to-all-done.1), kind=kLoop, calls=%fused_computation.3 | loop fusion | flops 983040 | bytes 2621440 | tf_op jit(solution)/shard_map/reduce_sum | solution.py:93
  159.0 2.9 %reshape.237 = f32[80,4096]{1,0:T(8,128)} reshape(f32[16,5,4096]{2,1,0:T(8,128)} %convert_reduce_fusion) | data formatting | bytes 2621440 | tf_op jit(solution)/shard_map/reshape | solution.py:93
  161.9 0.0 copy-start.2
  161.9 3.6 %gather_fusion.1 = f32[64,4096]{1,0:T(8,128)} fusion(f32[80,4096]{1,0:T(8,128)} %reshape.237, s32[1024]{0:T(1024)S(1)} %pad_clamp_fusion), kind=kCustom, calls=%fused_computation.1 | custom fusion | bytes 2097408 | tf_op jit(solution)/shard_map/gather | solution.py:94
  165.6 0.0 copy-done.2
  165.6 2.2 %fusion.13 = bf16[8,4096]{1,0:T(8,128)(2,1)} fusion(f32[64,4096]{1,0:T(8,128)} %gather_fusion.1, f32[8,8]{1,0:T(8,128)S(1)} %copy-done.2), kind=kLoop, calls=%fused_computation.12 | loop fusion | flops 491520 | bytes 1114368 | tf_op jit(solution)/shard_map/reduce_sum | solution.py:95
  (10 shorter events, 0.1 us)
Async XLA Ops:
  0.6 73.3 %copy-start = (bf16[1,384,4096]{2,1,0:T(8,128)(2,1)S(1)}, bf16[1,384,4096]{2,1,0:T(8,128)(2,1)}, u32[]{:S(2)}) copy-start(bf16[1,384,4096]{2,1,0:T(8,128)(2,1)} %param.13) | copy-start | bytes 9437188
  81.6 3.8 %copy-start.1 = (s32[8,8]{1,0:T(8,128)S(1)}, s32[8,8]{1,0:T(8,128)}, u32[]{:S(2)}) copy-start(s32[8,8]{1,0:T(8,128)} %param.14) | copy-start | bytes 772
  81.6 73.8 %all-to-all-start.1 = ((bf16[32,5,4096]{2,1,0:T(8,128)(2,1)}), bf16[32,5,4096]{2,1,0:T(8,128)(2,1)}, u32[]{:S(2)}, u32[]{:S(2)}) async-start(bf16[32,5,4096]{2,1,0:T(8,128)(2,1)} %reshape.236), calls=%async_computation.1 | async-start | bytes 4194304 | tf_op jit(solution)/shard_map/all_to_all | solution.py:85
  161.9 3.7 %copy-start.2 = (f32[8,8]{1,0:T(8,128)S(1)}, f32[8,8]{1,0:T(8,128)}, u32[]{:S(2)}) copy-start(f32[8,8]{1,0:T(8,128)} %param.17) | copy-start | bytes 772
where the time goes:
time: 168 us
  blocking collectives  125 us (74%)
  local copies, waits for them, and re-layouts  19.8 us (12%)
  other arithmetic  10.6 us (6%)
  matrix products  8.15 us (5%)
  starting transfers between devices  3.79 us (2%)
    unnamed x1, blocking collectives  68.8 us
    all_to_all x1, blocking collectives, per_device(): lax.all_to_all(bucket, ('expert', 'dp'), split_axis=0, concat_axis=0, til...  55.9 us
    dot_general x1, matrix products, expert_block(): jnp.dot(hidden, down_piece, preferred_element_type=jnp.float32)  5.01 us
    gather x2, local copies, waits for them, and re-layouts, per_device(): normed[token_index]  4.14 us
    all_to_all x1, starting transfers between devices, per_device(): lax.all_to_all(result_rows.reshape(received.shape[0], received.shape[1],...  3.79 us
    gather x1, local copies, waits for them, and re-layouts, per_device(): per_assign = pair_result[row_index] * combine_weight.reshape(-1)[:, None]  3.65 us
    reduce_sum x1, other arithmetic, per_device(): pair_result = jnp.sum(pair_result, axis=1).reshape(bucket_rows, model_width)  3.57 us
  transfers between devices with their start and end apart: 1, of which 0 were waited for; matrix products, arithmetic and copies ran while one was open for 1% of the time, Pallas kernels for 0%

commit v1 on v0

v1 whole, which is shorter than its diff:
```python
import jax
import jax.numpy as jnp
from jax import lax
from jax.sharding import PartitionSpec as P


def plan(experts_chosen, replica_choice, replica_cols, combine_weight, pair_cols, pair_count):
    rep_count = replica_cols.shape[1]
    column = experts_chosen // pair_cols
    within = experts_chosen % pair_cols
    rows_hot = within[..., None] == jnp.arange(pair_cols, dtype=jnp.int32)
    home_col = jnp.sum(jnp.where(rows_hot, replica_cols[:, 0], 0), axis=-1)
    flat_hot = (within * rep_count + replica_choice)[..., None] == jnp.arange(
        pair_cols * rep_count, dtype=jnp.int32
    )
    chosen_col = jnp.sum(jnp.where(flat_hot, replica_cols.reshape(-1), 0), axis=-1)
    holder_col = jnp.where(column == home_col, chosen_col, column)
    plan_slot = (holder_col != column).astype(jnp.int32)
    plan_key = (holder_col * pair_cols + within) * 2 + plan_slot
    keys = jnp.arange(pair_count * 2, dtype=jnp.int32)
    counts = jnp.sum((plan_key[..., None] == keys).astype(jnp.float32), axis=1)
    experts = jnp.arange(pair_count, dtype=jnp.int32)
    weights = jnp.sum(
        jnp.where(experts_chosen[..., None] == experts, combine_weight[..., None], 0.0), axis=1
    )
    return counts, weights


def per_device(
    tokens,
    norm_gain,
    gate_weight,
    up_weight,
    down_weight,
    experts_chosen,
    replica_choice,
    replica_cols,
    combine_weight,
):
    expert_count = lax.axis_size("expert")
    dp_count = lax.axis_size("dp")
    axes = ("expert", "dp")
    pair_cols = dp_count // 2
    pair_count = expert_count * pair_cols
    tok_rows = tokens.shape[0]
    values = tokens.astype(jnp.float32)
    scale = lax.rsqrt(jnp.mean(values * values, axis=1, keepdims=True) + 1e-06)
    normed = (values * scale * norm_gain).astype(jnp.bfloat16)
    counts, weights = plan(
        experts_chosen, replica_choice, replica_cols, combine_weight, pair_cols, pair_count
    )
    side = jnp.concatenate([weights, counts], axis=1)
    side = lax.all_gather(side, axes, axis=0, tiled=True)
    rows = lax.all_gather(normed, axes, axis=0, tiled=True)
    pair = lax.axis_index("expert") * pair_cols + lax.axis_index("dp") // 2
    weight = lax.dynamic_slice_in_dim(side, pair, 1, axis=1)
    served = jnp.sum(lax.dynamic_slice_in_dim(side, pair_count + 2 * pair, 2, axis=1), axis=0)
    loads = (served / jnp.float32(tok_rows))[None, :]
    gate_out = jnp.dot(rows, gate_weight[0], preferred_element_type=jnp.float32)
    up_out = jnp.dot(rows, up_weight[0], preferred_element_type=jnp.float32)
    hidden = (jax.nn.silu(gate_out) * up_out).astype(jnp.bfloat16)
    out = jnp.dot(hidden, down_weight[0], preferred_element_type=jnp.float32) * weight
    mixed = lax.psum_scatter(out, axes, scatter_dimension=0, tiled=True).astype(jnp.bfloat16)
    return (mixed, loads)


def solution(mesh):
    rows = P(("groups", "expert", "dp"), None)
    pieces = P(("expert", "dp"), None, None)
    return jax.shard_map(
        per_device,
        mesh=mesh,
        in_specs=(rows, P(), pieces, pieces, pieces, rows, rows, P(), rows),
        out_specs=(rows, rows),
        check_vma=False,
    )
```

time: 168 us -> 231 us (1.38)
  waiting for transfers between devices: 0.01 us -> 152 us
  blocking collectives: 125 us -> 43.6 us
  local copies, waits for them, and re-layouts: 19.8 us -> 1.74 us
  between operations: 0.76 us -> 14.1 us
  starting transfers between devices: 3.79 us -> 0.08 us
  matrix products: 8.15 us -> 11.5 us
  other arithmetic: 10.6 us -> 7.61 us
    reduce_scatter x0 -> x1, waiting for transfers between devices: none -> 139 us  [per_device(): lax.psum_scatter(out, axes, scatter_dimension=0, tiled=True)]
    unnamed x1 -> x0, blocking collectives: 68.8 us -> none
    all_to_all x1 -> x0, blocking collectives: 55.9 us -> none  [per_device(): lax.all_to_all(bucket, ('expert', 'dp'), split_axis=0, concat_axis=0, til...]
    all_gather x0 -> x1, blocking collectives: none -> 43.6 us  [per_device(): side = lax.all_gather(side, axes, axis=0, tiled=True)]
    all_gather x0 -> x1, waiting for transfers between devices: none -> 12.5 us  [per_device(): rows = lax.all_gather(normed, axes, axis=0, tiled=True)]
    reshape x5 -> x1, local copies, waits for them, and re-layouts: 9.22 us -> 0.76 us  [plan(): replica_cols.reshape(-1)]
    gather x3 -> x0, local copies, waits for them, and re-layouts: 7.79 us -> none  [the longest x2 4.14 us: per_device(): normed[token_index]]
    reduce_sum x7 -> x5, other arithmetic: 7.04 us -> 1.35 us  [the longest x1 0.79 us: plan(): jnp.sum(jnp.where(experts_chosen[..., None] == experts, combine_weight[.....]
  transfers between devices with their start and end apart: 1 -> 2, of which waited for: 0 -> 2; matrix products, arithmetic and copies ran while one was open for 1% -> 2% of each run, Pallas kernels for 0% -> 0%
where the time goes in v1:
time: 231 us; the launch traced here: 230 us
  waiting for transfers between devices  152 us (66%)
  blocking collectives  43.6 us (19%)
  between operations  14.1 us (6%)
  matrix products  11.5 us (5%)
  other arithmetic  7.61 us (3%)
    reduce_scatter x1, waiting for transfers between devices, per_device(): lax.psum_scatter(out, axes, scatter_dimension=0, tiled=True)  139 us
    all_gather x1, blocking collectives, per_device(): side = lax.all_gather(side, axes, axis=0, tiled=True)  43.6 us
    all_gather x1, waiting for transfers between devices, per_device(): rows = lax.all_gather(normed, axes, axis=0, tiled=True)  12.5 us
    dot_general x1, matrix products, per_device(): jnp.dot(hidden, down_weight[0], preferred_element_type=jnp.float32) * weight  6.93 us
  transfers between devices with their start and end apart: 2, of which 2 were waited for; matrix products, arithmetic and copies ran while one was open for 2% of the time, Pallas kernels for 0%

profile of v1, /device:TPU:0, one launch (start us, length us, event | category | flops | bytes accessed | tf_op | source)
XLA Modules:
  0.0 230.2 jit_solution(3311564741516964418)
XLA Ops:
  7.2 0.0 copy-start
  7.2 0.0 all-gather.2.cloned.1.call-start
  7.2 1.1 fusion.19
  8.4 1.6 fusion.21
  9.9 0.0 all-gather.2.cloned.1.call-update
  10.0 0.0 reduce-scatter.2.cloned.1.call-start
  10.0 0.8 reshape.30
  10.8 0.8 slice_reduce_fusion
  11.6 0.7 add_select_fusion
  12.3 0.1 select_reduce_fusion.2
  12.4 0.3 select_reduce_fusion
  12.6 0.7 convert_add_fusion
  13.4 0.1 convert_reduce_fusion
  13.4 0.8 select_reduce_fusion.1
  14.2 0.1 pad_maximum_fusion
  14.3 43.6 %all_gather.7 = f32[256,48]{1,0:T(8,128)S(1)} all-gather(f32[8,48]{1,0:T(8,128)S(1)} %pad_maximum_fusion), channel_id=1, replica_groups=mesh['groups'=1,'expert'=8,'dp'=4] {'expert','dp'}, dimensions={0}, use_global_device_ids=true | all-gather | bytes 50688 | tf_op jit(solution)/shard_map/all_gather | solution.py:53
  58.0 0.2 dynamic-slice_reduce_fusion.1
  58.1 12.5 %all-gather.2.cloned.1.call-done = bf16[256,4096]{1,0:T(8,128)(2,1)} async-done(((bf16[8,4096]{1,0:T(8,128)(2,1)}), bf16[256,4096]{1,0:T(8,128)(2,1)}) %all-gather.2.cloned.1.call-update) | async-done | bytes 2097168 | tf_op jit(solution)/shard_map/all_gather | solution.py:54
  70.7 4.5 %fusion.3 = f32[256,384]{1,0:T(8,128)} fusion(bf16[256,4096]{1,0:T(8,128)(2,1)} %all-gather.2.cloned.1.call-done, bf16[1,4096,384]{2,1,0:T(8,128)(2,1)} %param.11), kind=kOutput, calls=%fused_computation.4 | convolution fusion | flops 805306368 | bytes 5636096 | tf_op jit(solution)/shard_map/dot_general | solution.py:59
  75.2 0.0 copy-done
  75.2 6.9 %convolution_multiply_fusion = f32[256,4096]{1,0:T(8,128)} fusion(bf16[1,384,4096]{2,1,0:T(8,128)(2,1)S(1)} %copy-done, f32[256]{0:T(256)S(1)} %dynamic-slice_reduce_fusion.1, bf16[256,4096]{1,0:T(8,128)(2,1)} %all-gather.2.cloned.1.call-done, bf16[1,4096,384]{2,1,0:T(8,128)(2,1)} %param.12, f32[256,384]{1,0:T(8,128)} %fusion.3), kind=kOutput, calls=%fused_computation | convolution fusion | flops 1612251136 | bytes 12977152 | tf_op jit(solution)/shard_map/dot_general | solution.py:62
  82.1 0.0 reduce-scatter.2.cloned.1.call-update
  82.2 0.1 dynamic-slice_reduce_fusion
  82.3 0.5 multiply_bitcast_fusion
  82.8 139.1 %reduce-scatter.2.cloned.1.call-done = f32[8,4096]{1,0:T(8,128)} async-done(((f32[256,4096]{1,0:T(8,128)}), f32[8,4096]{1,0:T(8,128)}) %reduce-scatter.2.cloned.1.call-update) | async-done | bytes 131088 | tf_op jit(solution)/shard_map/reduce_scatter | solution.py:63
  221.9 1.5 convert_element_type.23
  (1 shorter events, 0.0 us)
Async XLA Ops:
  7.2 68.0 %copy-start = (bf16[1,384,4096]{2,1,0:T(8,128)(2,1)S(1)}, bf16[1,384,4096]{2,1,0:T(8,128)(2,1)}, u32[]{:S(2)}) copy-start(bf16[1,384,4096]{2,1,0:T(8,128)(2,1)} %param.13) | copy-start | bytes 9437188
  7.2 63.5 %all-gather.2.cloned.1.call-start = ((), (), s32[]{:S(2)}) async-start(), calls=%async_computation.1 | async-start | bytes 2162688 | tf_op jit(solution)/shard_map/all_gather | solution.py:54
  10.0 211.9 %reduce-scatter.2.cloned.1.call-start = ((), (), s32[]{:S(2)}) async-start(), calls=%async_computation.2 | async-start | bytes 4325376 | tf_op jit(solution)/shard_map/reduce_scatter | solution.py:63
Sparse Core Ops, SparseCore 0:
  11.4 59.1 all-gather.1
  82.3 139.5 reduce-scatter.1

commit v2 on v1

--- a/solution.py
+++ b/solution.py
@@ -1,7 +1,16 @@
+import functools
+
 import jax
 import jax.numpy as jnp
 from jax import lax
+from jax.experimental import pallas as pl
+from jax.experimental.pallas import tpu as pltpu
 from jax.sharding import PartitionSpec as P
+
+MESH = pl.DeviceIdType.MESH
+LANES = 128
+BF16 = jnp.bfloat16
+F32 = jnp.float32
 
 
 def plan(experts_chosen, replica_choice, replica_cols, combine_weight, pair_cols, pair_count):
@@ -24,6 +33,322 @@
         jnp.where(experts_chosen[..., None] == experts, combine_weight[..., None], 0.0), axis=1
     )
     return counts, weights
+
+
+def fused_kernel(
+    depth, rep_count, tokens_ref, gain_ref, chosen_ref, choice_ref, cols_ref, combine_ref,
+    gate_hbm, up_hbm, down_hbm, mixed_ref, loads_ref,
+    gate_v, up_v, down_v, swap_out, swap_in, g0, g1, gate_acc, up_acc, hidden_v,
+    s1, r1, own, s2, r2, s3, r3, f_out, f_in,
+    load_sem, pair_send, pair_recv, z_send, z_recv, a1_send, a1_recv, a2_send, a2_recv,
+    sib_send, sib_recv, c1_send, c1_recv, c2_send, c2_recv, c3_send, c3_recv,
+):
+    grow = (g0, g1)
+    tok_rows, width = tokens_ref.shape
+    half, quarter = width // 2, width // 4
+    ff = gate_v.shape[1]
+    experts = depth * 4
+    expert, dp = lax.axis_index("expert"), lax.axis_index("dp")
+    z, y, x, c = expert // 2, expert % 2, dp // 2, dp % 2
+    chip = expert * 2 + x
+    here = y * 2 + x
+    cat = (here, y * 2 + 1 - x, (1 - y) * 2 + x, (1 - y) * 2 + 1 - x)
+    sibling = {"expert": expert, "dp": x * 2 + 1 - c}
+    x_next = {"expert": expert, "dp": (1 - x) * 2 + c}
+    y_next = {"expert": z * 2 + 1 - y, "dp": dp}
+    near = (x_next, y_next)
+
+    def z_at(step):
+        return {"expert": lax.rem(z + step, depth) * 2 + y, "dp": dp}
+
+    sends = []
+
+    def send(src, dst, send_sem, recv_sem, device):
+        copy = pltpu.make_async_remote_copy(
+            src_ref=src, dst_ref=dst, send_sem=send_sem, recv_sem=recv_sem,
+            device_id=device, device_id_type=MESH,
+        )
+        copy.start()
+        sends.append(copy)
+
+    def arrived(ref, send_sem, recv_sem):
+        pltpu.make_async_remote_copy(
+            src_ref=ref, dst_ref=ref, send_sem=send_sem, recv_sem=recv_sem,
+            device_id=sibling, device_id_type=MESH,
+        ).wait_recv()
+
+    loads_in = [
+        pltpu.make_async_copy(gate_hbm.at[0], gate_v, load_sem.at[0]),
+        pltpu.make_async_copy(up_hbm.at[0], up_v, load_sem.at[1]),
+        pltpu.make_async_copy(
+            down_hbm.at[0, :, pl.ds(pl.multiple_of(c * half, half), half)],
+            down_v.at[c], load_sem.at[2],
+        ),
+    ]
+    for copy in loads_in:
+        copy.start()
+
+    barrier = pltpu.get_barrier_semaphore()
+    partners = [sibling, x_next, y_next] + [z_at(step) for step in range(1, depth)]
+    for partner in partners:
+        pl.semaphore_signal(barrier, inc=1, device_id=partner, device_id_type=MESH)
+
+    values = tokens_ref[...].astype(F32)
+    scale = lax.rsqrt(jnp.mean(values * values, axis=1, keepdims=True) + 1e-06)
+    normed = (values * scale * gain_ref[...]).astype(BF16).astype(F32)
+    lane = lax.broadcasted_iota(jnp.int32, (tok_rows, LANES), 1)
+    side = jnp.zeros((tok_rows, LANES), F32)
+    for k in range(chosen_ref.shape[1]):
+        name = chosen_ref[:, k : k + 1]
+        pick = choice_ref[:, k : k + 1]
+        odd = (name & 1) == 1
+        home = jnp.where(odd, cols_ref[1, 0], cols_ref[0, 0])
+        holder = jnp.zeros_like(name)
+        for r in range(rep_count):
+            holder = jnp.where(pick == r, jnp.where(odd, cols_ref[1, r], cols_ref[0, r]), holder)
+        column = name >> 1
+        holder = jnp.where(column == home, holder, column)
+        slot = jnp.where(holder == column, 0, 1)
+        key = (holder * 2 + (name & 1)) * 2 + slot
+        weight = combine_ref[:, k : k + 1]
+        named = (lane == name) | (lane == name + experts)
+        side = side + jnp.where(named, weight, 0.0)
+        side = side + jnp.where(lane == key + 2 * experts, 1.0, 0.0)
+    left, right = normed[:, :half], normed[:, half:]
+    mine = jnp.where(c == 0, left, right)
+    swap_out[:, :half] = jnp.where(c == 0, right, left)
+    swap_out[:, half:] = side
+
+    pl.semaphore_wait(barrier, len(partners))
+    send(swap_out, swap_in, pair_send.at[0], pair_recv.at[0], sibling)
+    send(
+        down_hbm.at[0, :, pl.ds(pl.multiple_of((1 - c) * half, half), half)],
+        down_v.at[c], pair_send.at[1], pair_recv.at[1], sibling,
+    )
+    arrived(swap_in, pair_send.at[0], pair_recv.at[0])
+    other = swap_in[:, :half]
+    rows = jnp.concatenate(
+        [jnp.where(c == 0, mine, other), jnp.where(c == 0, other, mine)], axis=0
+    ).astype(BF16)
+    other_side = swap_in[:, half:]
+    side = jnp.concatenate(
+        [jnp.where(c == 0, side, other_side), jnp.where(c == 0, other_side, side)], axis=0
+    )
+    lanes = lax.broadcasted_iota(jnp.int32, side.shape, 1)
+    low = (lanes >= experts) & (lanes < 2 * experts)
+    side = jnp.where(low, side - side.astype(BF16).astype(F32), side).astype(BF16)
+    g0[c, here, z, :, :quarter] = rows[:, :quarter]
+    g0[c, here, z, :, quarter:] = side
+    g1[c, here, z] = rows[:, quarter:]
+
+    def block(q, place, step):
+        return grow[q].at[c, place, lax.rem(z - step + depth, depth)]
+
+    def to_sibling(q, kind, step):
+        ref = block(q, cat[kind], step)
+        send(ref, ref, sib_send.at[q, kind, step], sib_recv.at[q, kind, step], sibling)
+
+    def spread(step):
+        for q in range(2):
+            ref = block(q, here, step)
+            send(ref, ref, a1_send.at[q, step], a1_recv.at[q, step], near[q])
+        for q in range(2):
+            ref = block(q, here, step)
+            send(ref, ref, a2_send.at[q, 0, step], a2_recv.at[q, 0, step], near[1 - q])
+            to_sibling(q, 0, step)
+
+    def forward(step):
+        for q in range(2):
+            ref = block(q, cat[1 + q], step)
+            arrived(ref, a1_send.at[q, step], a1_recv.at[q, step])
+            send(ref, ref, a2_send.at[q, 1, step], a2_recv.at[q, 1, step], near[1 - q])
+            to_sibling(q, 1 + q, step)
+
+    for step in range(1, depth):
+        for q in range(2):
+            ref = block(q, here, 0)
+            send(ref, ref, z_send.at[q, step], z_recv.at[q, step], z_at(step))
+    spread(0)
+    for step in range(1, depth):
+        for q in range(2):
+            arrived(block(q, here, step), z_send.at[q, step], z_recv.at[q, step])
+        spread(step)
+        forward(step - 1)
+    forward(depth - 1)
+    for step in range(depth):
+        for q in range(2):
+            for j in range(2):
+                kind = 3 if j == 1 else 2 - q
+                arrived(block(q, cat[kind], step), a2_send.at[q, j, step], a2_recv.at[q, j, step])
+                to_sibling(q, kind, step)
+
+    all_rows = 4 * depth * 2 * tok_rows
+    for copy in loads_in:
+        copy.wait()
+
+    def project(h, first):
+        for q in range(2):
+            block_rows = grow[q][h, :, :, :, :quarter].reshape(all_rows, quarter)
+            at = pl.ds(pl.multiple_of(h * half + q * quarter, quarter), quarter)
+            gate = jnp.dot(block_rows, gate_v[at, :], preferred_element_type=F32)
+            up = jnp.dot(block_rows, up_v[at, :], preferred_element_type=F32)
+            if first and q == 0:
+                gate_acc[...] = gate
+                up_acc[...] = up
+            else:
+                gate_acc[...] += gate
+                up_acc[...] += up
+
+    project(c, True)
+    for step in range(depth):
+        for q in range(2):
+            for kind in range(4):
+                ref = grow[q].at[1 - c, cat[kind], lax.rem(z - step + depth, depth)]
+                arrived(ref, sib_send.at[q, kind, step], sib_recv.at[q, kind, step])
+    project(1 - c, False)
+    gate = gate_acc[...]
+    hidden = gate * (1.0 / (1.0 + jnp.exp(-gate))) * up_acc[...]
+    hidden_v[c] = hidden.astype(BF16)
+    send(hidden_v.at[c], hidden_v.at[c], pair_send.at[2], pair_recv.at[2], sibling)
+
+    meta = g0[c, :, :, :, quarter:].reshape(all_rows, LANES).astype(F32)
+    meta_lane = lax.broadcasted_iota(jnp.int32, meta.shape, 1)
+    ours = (meta_lane == chip) | (meta_lane == chip + experts)
+    weights = jnp.sum(jnp.where(ours, meta, 0.0), axis=1, keepdims=True)
+    gate_acc[:, :LANES] = jnp.broadcast_to(weights, (all_rows, LANES))
+    totals = jnp.sum(meta, axis=0, keepdims=True)
+    total_lane = lax.broadcasted_iota(jnp.int32, totals.shape, 1)
+    base = 2 * experts + 2 * chip
+    home_count = jnp.sum(jnp.where(total_lane == base, totals, 0.0), axis=1, keepdims=True)
+    copy_count = jnp.sum(jnp.where(total_lane == base + 1, totals, 0.0), axis=1, keepdims=True)
+    two = lax.broadcasted_iota(jnp.int32, (1, 2), 1)
+    loads_ref[...] = jnp.where(two == 0, home_count, copy_count) / tok_rows
+
+    arrived(down_v.at[1 - c], pair_send.at[1], pair_recv.at[1])
+    arrived(hidden_v.at[1 - c], pair_send.at[2], pair_recv.at[2])
+    line = depth * 2 * tok_rows
+
+    def line_rows(ref, place):
+        return ref[pl.ds(pl.multiple_of(place * line, line), line), :]
+
+    def outputs(q, places):
+        total = None
+        for p in range(2):
+            part = jnp.concatenate([line_rows(hidden_v.at[p], place) for place in places], axis=0)
+            at = slice(q * quarter, (q + 1) * quarter)
+            term = jnp.dot(part, down_v[p, :, at], preferred_element_type=F32)
+            total = term if total is None else total + term
+        factor = jnp.concatenate(
+            [line_rows(gate_acc, place)[:, :1] for place in places], axis=0
+        )
+        return (total * factor).reshape(2, depth, 2 * tok_rows, quarter)
+
+    back = (y_next, x_next)
+    order = list(range(1, depth)) + [0]
+    for q in range(2):
+        far = (cat[3], cat[2 - q])
+        s1[q] = outputs(q, far).astype(BF16)
+        for j in range(2):
+            for step in order:
+                to = lax.rem(z + step, depth)
+                send(
+                    s1.at[q, j, to], r1.at[q, j, to],
+                    c1_send.at[q, j, step], c1_recv.at[q, j, step], back[q],
+                )
+    for q in range(2):
+        own[q] = outputs(q, (cat[1 + q], here))
+    for step in order:
+        for q in range(2):
+            to = lax.rem(z + step, depth)
+            arrived(r1.at[q, 0, to], c1_send.at[q, 0, step], c1_recv.at[q, 0, step])
+            s2[q, to] = (own[q, 0, to] + r1[q, 0, to].astype(F32)).astype(BF16)
+            send(
+                s2.at[q, to], r2.at[q, to],
+                c2_send.at[q, step], c2_recv.at[q, step], back[1 - q],
+            )
+    for step in order:
+        for q in range(2):
+            to = lax.rem(z + step, depth)
+            arrived(r1.at[q, 1, to], c1_send.at[q, 1, step], c1_recv.at[q, 1, step])
+            arrived(r2.at[q, to], c2_send.at[q, step], c2_recv.at[q, step])
+            value = own[q, 1, to] + r1[q, 1, to].astype(F32) + r2[q, to].astype(F32)
+            if step == 0:
+                own[q, 1, to] = value
+            else:
+                s3[q, step] = value.astype(BF16)
+                send(
+                    s3.at[q, step], r3.at[q, step],
+                    c3_send.at[q, step], c3_recv.at[q, step], z_at(step),
+                )
+    kept = []
+    for q in range(2):
+        value = own[q, 1, z]
+        for step in range(1, depth):
+            arrived(r3.at[q, step], c3_send.at[q, step], c3_recv.at[q, step])
+            value = value + r3[q, step].astype(F32)
+        top, bottom = value[:tok_rows], value[tok_rows:]
+        f_out[q] = jnp.where(c == 0, bottom, top)
+        kept.append(jnp.where(c == 0, top, bottom))
+    send(f_out, f_in, pair_send.at[3], pair_recv.at[3], sibling)
+    arrived(f_in, pair_send.at[3], pair_recv.at[3])
+    for q in range(2):
+        there = f_in[q]
+        for h in range(2):
+            mixed_ref[:, h * half + q * quarter : h * half + (q + 1) * quarter] = jnp.where(
+                c == h, kept[q], there
+            ).astype(BF16)
+    for copy in sends:
+        copy.wait_send()
+
+
+def fused(tokens, norm_gain, gate, up, down, chosen, choice, cols, combine):
+    tok_rows, width = tokens.shape
+    ff = gate.shape[2]
+    depth = lax.axis_size("expert") // 2
+    half, quarter, pair_rows = width // 2, width // 4, 2 * tok_rows
+    rows = 4 * depth * pair_rows
+    vmem = pl.BlockSpec(memory_space=pltpu.VMEM)
+    smem = pl.BlockSpec(memory_space=pltpu.SMEM)
+    anywhere = pl.BlockSpec(memory_space=pl.ANY)
+    dma = pltpu.SemaphoreType.DMA
+    return pl.pallas_call(
+        functools.partial(fused_kernel, depth, cols.shape[1]),
+        out_shape=(
+            jax.ShapeDtypeStruct((tok_rows, width), BF16),
+            jax.ShapeDtypeStruct((1, 2), F32),
+        ),
+        in_specs=[vmem, vmem, vmem, vmem, smem, vmem, anywhere, anywhere, anywhere],
+        out_specs=(vmem, vmem),
+        scratch_shapes=[
+            pltpu.VMEM((width, ff), BF16),
+            pltpu.VMEM((width, ff), BF16),
+            pltpu.VMEM((2, ff, half), BF16),
+            pltpu.VMEM((tok_rows, half + LANES), F32),
+            pltpu.VMEM((tok_rows, half + LANES), F32),
+            pltpu.VMEM((2, 4, depth, pair_rows, quarter + LANES), BF16),
+            pltpu.VMEM((2, 4, depth, pair_rows, quarter), BF16),
+            pltpu.VMEM((rows, ff), F32),
+            pltpu.VMEM((rows, ff), F32),
+            pltpu.VMEM((2, rows, ff), BF16),
+            pltpu.VMEM((2, 2, depth, pair_rows, quarter), BF16),
+            pltpu.VMEM((2, 2, depth, pair_rows, quarter), BF16),
+            pltpu.VMEM((2, 2, depth, pair_rows, quarter), F32),
+            pltpu.VMEM((2, depth, pair_rows, quarter), BF16),
+            pltpu.VMEM((2, depth, pair_rows, quarter), BF16),
+            pltpu.VMEM((2, depth, pair_rows, quarter), BF16),
+            pltpu.VMEM((2, depth, pair_rows, quarter), BF16),
+            pltpu.VMEM((2, tok_rows, quarter), F32),
+            pltpu.VMEM((2, tok_rows, quarter), F32),
+            dma((3,)), dma((4,)), dma((4,)),
+            dma((2, depth)), dma((2, depth)), dma((2, depth)), dma((2, depth)),
+            dma((2, 2, depth)), dma((2, 2, depth)), dma((2, 4, depth)), dma((2, 4, depth)),
+            dma((2, 2, depth)), dma((2, 2, depth)), dma((2, depth)), dma((2, depth)),
+            dma((2, depth)), dma((2, depth)),
+        ],
+        compiler_params=pltpu.CompilerParams(
+            collective_id=0, has_side_effects=True, vmem_limit_bytes=56 * 1024 * 1024
+        ),
+    )(tokens, norm_gain.reshape(1, width), chosen, choice, cols, combine, gate, up, down)
 
 
 def per_device(
@@ -40,6 +365,11 @@
     expert_count = lax.axis_size("expert")
     dp_count = lax.axis_size("dp")
     axes = ("expert", "dp")
+    if dp_count == 4 and expert_count % 2 == 0 and expert_count * 8 <= LANES:
+        return fused(
+            tokens, norm_gain, gate_weight, up_weight, down_weight,
+            experts_chosen, replica_choice, replica_cols, combine_weight,
+        )
     pair_cols = dp_count // 2
     pair_count = expert_count * pair_cols
     tok_rows = tokens.shape[0]

time: 231 us -> 48.7 us (0.21)
  waiting for transfers between devices: 152 us -> 0 us
  Pallas kernels: 0 us -> 45.1 us
  blocking collectives: 43.6 us -> 0 us
  between operations: 14.1 us -> 0.64 us
  matrix products: 11.5 us -> 0 us
  other arithmetic: 7.61 us -> 0 us
    reduce_scatter x1 -> x0, waiting for transfers between devices: 139 us -> none  [per_device(): lax.psum_scatter(out, axes, scatter_dimension=0, tiled=True)]
    pallas_call x0 -> x1, Pallas kernels: none -> 45.1 us  [fused(): pl.pallas_call(functools.partial(fused_kernel, depth, cols.shape[1]), out...]
    all_gather x1 -> x0, blocking collectives: 43.6 us -> none  [per_device(): side = lax.all_gather(side, axes, axis=0, tiled=True)]
    all_gather x1 -> x0, waiting for transfers between devices: 12.5 us -> none  [per_device(): rows = lax.all_gather(normed, axes, axis=0, tiled=True)]
    dot_general x2 -> x0, matrix products: 11.5 us -> none  [the longest x1 6.93 us: per_device(): jnp.dot(hidden, down_weight[0], preferred_element_type=jnp.float32) * weight]
    convert_element_type x2 -> x0, other arithmetic: 3.1 us -> none  [the longest x1 1.56 us: per_device(): normed = (values * scale * norm_gain).astype(jnp.bfloat16)]
    unnamed x2, local copies, waits for them, and re-layouts: 0.01 us -> 2.59 us
    reduce_sum x6 -> x0, other arithmetic: 2.49 us -> none  [the longest x1 1.14 us: per_device(): scale = lax.rsqrt(jnp.mean(values * values, axis=1, keepdims=True) + 1e-06)]
  transfers between devices with their start and end apart: 2 -> 0, of which waited for: 2 -> 0; matrix products, arithmetic and copies ran while one was open for 2% -> 0% of each run, Pallas kernels for 0% -> 0%
where the time goes in v2:
time: 48.7 us; the launch traced here: 48.4 us
  Pallas kernels  45.1 us (93%)
  local copies, waits for them, and re-layouts  2.59 us (5%)
  between operations  0.64 us (1%)
    pallas_call x1, Pallas kernels, fused(): pl.pallas_call(functools.partial(fused_kernel, depth, cols.shape[1]), out...  45.1 us
    unnamed x2, local copies, waits for them, and re-layouts  2.59 us

profile of v2, /device:TPU:0, one launch (start us, length us, event | category | flops | bytes accessed | tf_op | source)
XLA Modules:
  0.0 48.4 jit_solution(9455398948555099047)
XLA Ops:
  0.6 45.1 %shard_map.104 = (bf16[8,4096]{1,0:T(8,128)(2,1)}, f32[1,2]{1,0:T(1,128)}) custom-call(bf16[8,4096]{1,0:T(8,128)(2,1)} %tokens_ref.1, f32[1,4096]{1,0:T(1,128)} %bitcast.1, s32[8,8]{1,0:T(8,128)} %chosen_ref.1, s32[8,8]{1,0:T(8,128)} %choice_ref.1, s32[2,4]{1,0:T(2,128)} %cols_ref.1, f32[8,8]{1,0:T(8,128)} %combine_ref.1, bf16[1,4096,384]{2,1,0:T(8,128)(2,1)} %gate_hbm.1, ...), custom_call_target="tpu_custom_call" | custom-call | tf_op jit(solution)/shard_map/pallas_call | solution.py:314
  45.8 1.5 %copy.13 = bf16[8,4096]{1,0:T(8,128)(2,1)} copy(bf16[8,4096]{1,0:T(8,128)(2,1)} %get-tuple-element.4) | data formatting | bytes 131072
  47.3 1.1 %copy.14 = f32[1,2]{1,0:T(1,128)} copy(f32[1,2]{1,0:T(1,128)} %get-tuple-element.5) | data formatting | bytes 16

commit v3 on v2

--- a/solution.py
+++ b/solution.py
@@ -244,17 +244,19 @@
         return (total * factor).reshape(2, depth, 2 * tok_rows, quarter)
 
     back = (y_next, x_next)
+    def first_hop(q, j, step):
+        to = lax.rem(z + step, depth)
+        send(
+            s1.at[q, j, to], r1.at[q, j, to],
+            c1_send.at[q, j, step], c1_recv.at[q, j, step], back[q],
+        )
+
     order = list(range(1, depth)) + [0]
     for q in range(2):
         far = (cat[3], cat[2 - q])
         s1[q] = outputs(q, far).astype(BF16)
-        for j in range(2):
-            for step in order:
-                to = lax.rem(z + step, depth)
-                send(
-                    s1.at[q, j, to], r1.at[q, j, to],
-                    c1_send.at[q, j, step], c1_recv.at[q, j, step], back[q],
-                )
+        for step in order:
+            first_hop(q, 0, step)
     for q in range(2):
         own[q] = outputs(q, (cat[1 + q], here))
     for step in order:
@@ -266,6 +268,8 @@
                 s2.at[q, to], r2.at[q, to],
                 c2_send.at[q, step], c2_recv.at[q, step], back[1 - q],
             )
+        for q in range(2):
+            first_hop(q, 1, step)
     for step in order:
         for q in range(2):
             to = lax.rem(z + step, depth)
@@ -301,6 +305,11 @@
         copy.wait_send()
 
 
+def hand_out(mixed_in, loads_in, mixed_ref, loads_ref):
+    mixed_ref[...] = mixed_in[...]
+    loads_ref[...] = loads_in[...]
+
+
 def fused(tokens, norm_gain, gate, up, down, chosen, choice, cols, combine):
     tok_rows, width = tokens.shape
     ff = gate.shape[2]
@@ -311,7 +320,7 @@
     smem = pl.BlockSpec(memory_space=pltpu.SMEM)
     anywhere = pl.BlockSpec(memory_space=pl.ANY)
     dma = pltpu.SemaphoreType.DMA
-    return pl.pallas_call(
+    mixed, loads = pl.pallas_call(
         functools.partial(fused_kernel, depth, cols.shape[1]),
         out_shape=(
             jax.ShapeDtypeStruct((tok_rows, width), BF16),
@@ -349,6 +358,15 @@
             collective_id=0, has_side_effects=True, vmem_limit_bytes=56 * 1024 * 1024
         ),
     )(tokens, norm_gain.reshape(1, width), chosen, choice, cols, combine, gate, up, down)
+    return pl.pallas_call(
+        hand_out,
+        out_shape=(
+            jax.ShapeDtypeStruct((tok_rows, width), BF16),
+            jax.ShapeDtypeStruct((1, 2), F32),
+        ),
+        in_specs=[vmem, vmem],
+        out_specs=(vmem, vmem),
+    )(mixed, loads)
 
 
 def per_device(

time: 48.7 us -> 46.6 us (0.957)
  local copies, waits for them, and re-layouts: 2.59 us -> 0 us
  Pallas kernels: 45.1 us -> 45.6 us
    unnamed x2 -> x0, local copies, waits for them, and re-layouts: 2.59 us -> none
    pallas_call x0 -> x1, Pallas kernels: none -> 1.48 us  [fused(): pl.pallas_call(hand_out, out_shape=(jax.ShapeDtypeStruct((tok_rows, width...]
    pallas_call x1, Pallas kernels: 45.1 us -> 44.2 us  [fused(): pl.pallas_call(functools.partial(fused_kernel, depth, cols.shape[1]), out...]
where the time goes in v3:
time: 46.6 us; the launch traced here: 46.3 us
  Pallas kernels  45.6 us (98%)
  between operations  0.64 us (1%)
    pallas_call x1, Pallas kernels, fused(): pl.pallas_call(functools.partial(fused_kernel, depth, cols.shape[1]), out...  44.2 us
    pallas_call x1, Pallas kernels, fused(): pl.pallas_call(hand_out, out_shape=(jax.ShapeDtypeStruct((tok_rows, width...  1.48 us

profile of v3, /device:TPU:0, one launch (start us, length us, event | category | flops | bytes accessed | tf_op | source)
XLA Modules:
  0.0 46.3 jit_solution(2913468680380112949)
XLA Ops:
  0.6 44.2 %shard_map.104 = (bf16[8,4096]{1,0:T(8,128)(2,1)}, f32[1,2]{1,0:T(1,128)}) custom-call(bf16[8,4096]{1,0:T(8,128)(2,1)} %tokens_ref.1, f32[1,4096]{1,0:T(1,128)} %bitcast.1, s32[8,8]{1,0:T(8,128)} %chosen_ref.1, s32[8,8]{1,0:T(8,128)} %choice_ref.1, s32[2,4]{1,0:T(2,128)} %cols_ref.1, f32[8,8]{1,0:T(8,128)} %combine_ref.1, bf16[1,4096,384]{2,1,0:T(8,128)(2,1)} %gate_hbm.1, ...), custom_call_target="tpu_custom_call" | custom-call | tf_op jit(solution)/shard_map/pallas_call | solution.py:323
  44.8 1.5 %shard_map.105 = (bf16[8,4096]{1,0:T(8,128)(2,1)}, f32[1,2]{1,0:T(1,128)}) custom-call(bf16[8,4096]{1,0:T(8,128)(2,1)} %get-tuple-element.4.mixed_in, f32[1,2]{1,0:T(1,128)} %get-tuple-element.5.loads_in), custom_call_target="tpu_custom_call" | custom-call | tf_op jit(solution)/shard_map/pallas_call | solution.py:361

commit v4 on v3

--- a/solution.py
+++ b/solution.py
@@ -39,7 +39,7 @@
     depth, rep_count, tokens_ref, gain_ref, chosen_ref, choice_ref, cols_ref, combine_ref,
     gate_hbm, up_hbm, down_hbm, mixed_ref, loads_ref,
     gate_v, up_v, down_v, swap_out, swap_in, g0, g1, gate_acc, up_acc, hidden_v,
-    s1, r1, own, s2, r2, s3, r3, f_out, f_in,
+    s1, r1, own, s2, r2, s3, r3,
     load_sem, pair_send, pair_recv, z_send, z_recv, a1_send, a1_recv, a2_send, a2_recv,
     sib_send, sib_recv, c1_send, c1_recv, c2_send, c2_recv, c3_send, c3_recv,
 ):
@@ -61,6 +61,9 @@
     def z_at(step):
         return {"expert": lax.rem(z + step, depth) * 2 + y, "dp": dp}
 
+    def core_at(step, core):
+        return {"expert": lax.rem(z + step, depth) * 2 + y, "dp": x * 2 + core}
+
     sends = []
 
     def send(src, dst, send_sem, recv_sem, device):
@@ -90,6 +93,7 @@
 
     barrier = pltpu.get_barrier_semaphore()
     partners = [sibling, x_next, y_next] + [z_at(step) for step in range(1, depth)]
+    partners += [core_at(step, 1 - c) for step in range(1, depth)]
     for partner in partners:
         pl.semaphore_signal(barrier, inc=1, device_id=partner, device_id_type=MESH)
 
@@ -271,35 +275,36 @@
         for q in range(2):
             first_hop(q, 1, step)
     for step in order:
+        values = []
         for q in range(2):
             to = lax.rem(z + step, depth)
             arrived(r1.at[q, 1, to], c1_send.at[q, 1, step], c1_recv.at[q, 1, step])
             arrived(r2.at[q, to], c2_send.at[q, step], c2_recv.at[q, step])
-            value = own[q, 1, to] + r1[q, 1, to].astype(F32) + r2[q, to].astype(F32)
-            if step == 0:
-                own[q, 1, to] = value
+            values.append(own[q, 1, to] + r1[q, 1, to].astype(F32) + r2[q, to].astype(F32))
+        for k in range(2):
+            core = c if k == 0 else 1 - c
+            part = jnp.concatenate(
+                [jnp.where(core == 0, v[:tok_rows], v[tok_rows:]) for v in values], axis=0
+            )
+            if k == 0 and step == 0:
+                kept = part
             else:
-                s3[q, step] = value.astype(BF16)
+                s3[k, step] = part.astype(BF16)
                 send(
-                    s3.at[q, step], r3.at[q, step],
-                    c3_send.at[q, step], c3_recv.at[q, step], z_at(step),
+                    s3.at[k, step], r3.at[k, step],
+                    c3_send.at[k, step], c3_recv.at[k, step], core_at(step, core),
                 )
-    kept = []
+    sums = [kept, jnp.zeros_like(kept)]
+    for step in order:
+        for k in range(2):
+            if k == 1 or step != 0:
+                arrived(r3.at[k, step], c3_send.at[k, step], c3_recv.at[k, step])
+                sums[k] = sums[k] + r3[k, step].astype(F32)
     for q in range(2):
-        value = own[q, 1, z]
-        for step in range(1, depth):
-            arrived(r3.at[q, step], c3_send.at[q, step], c3_recv.at[q, step])
-            value = value + r3[q, step].astype(F32)
-        top, bottom = value[:tok_rows], value[tok_rows:]
-        f_out[q] = jnp.where(c == 0, bottom, top)
-        kept.append(jnp.where(c == 0, top, bottom))
-    send(f_out, f_in, pair_send.at[3], pair_recv.at[3], sibling)
-    arrived(f_in, pair_send.at[3], pair_recv.at[3])
-    for q in range(2):
-        there = f_in[q]
+        same, there = [total[q * tok_rows : (q + 1) * tok_rows] for total in sums]
         for h in range(2):
             mixed_ref[:, h * half + q * quarter : h * half + (q + 1) * quarter] = jnp.where(
-                c == h, kept[q], there
+                c == h, same, there
             ).astype(BF16)
     for copy in sends:
         copy.wait_send()
@@ -346,9 +351,7 @@
             pltpu.VMEM((2, depth, pair_rows, quarter), BF16),
             pltpu.VMEM((2, depth, pair_rows, quarter), BF16),
             pltpu.VMEM((2, depth, pair_rows, quarter), BF16),
-            pltpu.VMEM((2, tok_rows, quarter), F32),
-            pltpu.VMEM((2, tok_rows, quarter), F32),
-            dma((3,)), dma((4,)), dma((4,)),
+            dma((3,)), dma((3,)), dma((3,)),
             dma((2, depth)), dma((2, depth)), dma((2, depth)), dma((2, depth)),
             dma((2, 2, depth)), dma((2, 2, depth)), dma((2, 4, depth)), dma((2, 4, depth)),
             dma((2, 2, depth)), dma((2, 2, depth)), dma((2, depth)), dma((2, depth)),

time: 46.6 us -> 45.6 us (0.979)
  Pallas kernels: 45.6 us -> 44.2 us
    pallas_call x1, Pallas kernels: 44.2 us -> 42.7 us  [fused(): pl.pallas_call(functools.partial(fused_kernel, depth, cols.shape[1]), out...]
where the time goes in v4:
time: 45.6 us; the launch traced here: 44.8 us
  Pallas kernels  44.2 us (97%)
  between operations  0.64 us (1%)
    pallas_call x1, Pallas kernels, fused(): pl.pallas_call(functools.partial(fused_kernel, depth, cols.shape[1]), out...  42.7 us
    pallas_call x1, Pallas kernels, fused(): pl.pallas_call(hand_out, out_shape=(jax.ShapeDtypeStruct((tok_rows, width...  1.48 us

profile of v4, /device:TPU:0, one launch (start us, length us, event | category | flops | bytes accessed | tf_op | source)
XLA Modules:
  0.0 44.8 jit_solution(12017586713161687941)
XLA Ops:
  0.6 42.7 %shard_map.104 = (bf16[8,4096]{1,0:T(8,128)(2,1)}, f32[1,2]{1,0:T(1,128)}) custom-call(bf16[8,4096]{1,0:T(8,128)(2,1)} %tokens_ref.1, f32[1,4096]{1,0:T(1,128)} %bitcast.1, s32[8,8]{1,0:T(8,128)} %chosen_ref.1, s32[8,8]{1,0:T(8,128)} %choice_ref.1, s32[2,4]{1,0:T(2,128)} %cols_ref.1, f32[8,8]{1,0:T(8,128)} %combine_ref.1, bf16[1,4096,384]{2,1,0:T(8,128)(2,1)} %gate_hbm.1, ...), custom_call_target="tpu_custom_call" | custom-call | tf_op jit(solution)/shard_map/pallas_call | solution.py:328
  43.3 1.5 %shard_map.105 = (bf16[8,4096]{1,0:T(8,128)(2,1)}, f32[1,2]{1,0:T(1,128)}) custom-call(bf16[8,4096]{1,0:T(8,128)(2,1)} %get-tuple-element.4.mixed_in, f32[1,2]{1,0:T(1,128)} %get-tuple-element.5.loads_in), custom_call_target="tpu_custom_call" | custom-call | tf_op jit(solution)/shard_map/pallas_call | solution.py:364
